TPU v7x, 256 devices: a whole 4x4x8 slice. The times are simulated.
256 devices in a mesh: wa: 32 (over x, y, core), an: 8 (over z).
Axes of the slice: x: 4, y: 4, z: 8, core: 2. Of those that a mesh axis runs over, the one named last changes fastest.
Arguments:
- tensor: float32 [256, 1024, 128, 4], P('wa', None, 'an'), may hold values from -6 to 6
- factor_two: float32 [1024, 64], P('wa'), may hold values from -0.1875 to 0.1875
- factor_three: float32 [128, 64], P('an'), may hold values from -0.5 to 0.5
- factor_four: float32 [4, 2], replicated, may hold values from -3 to 3
- start_basis: float32 [256, 64], P('wa'), may hold values from -0.375 to 0.375
Outputs:
- scaled_factor: float32 [256, 64], P('wa')
All inputs are finite; a program needn't handle non-finite values.
Results may differ from a plain program's by a relative error of at most 0.00024.
Values sent between devices are 32-bit elements; how exact they have to be, the bound alone decides.
A program may use at most 64 MiB of HBM per device.

v0:
```python
import math

import jax
import jax.numpy as jnp
from jax import lax
from jax.sharding import PartitionSpec as P

RANK = 64
RANK_FOUR = 2
ITERS = 4


def per_device(tensor, factor_two, factor_three, factor_four, start_basis):
    highest = lax.Precision.HIGHEST
    full_two, basis = (
        lax.all_gather(factor_two, "wa", axis=0, tiled=True),
        lax.all_gather(start_basis, "wa", axis=0, tiled=True),
    )
    first = jnp.einsum("abcd,be->aecd", tensor, full_two, precision=highest)
    second = jnp.einsum("aecd,cf->aefd", first, factor_three, precision=highest)
    core = jnp.einsum("aefd,dg->aefg", second, factor_four, precision=highest)
    unfold = core.reshape(core.shape[0], -1)
    shares = lax.psum_scatter(unfold, "an", scatter_dimension=1, tiled=True)
    regrouped = lax.all_to_all(shares, "wa", split_axis=1, concat_axis=0, tiled=True)
    factor_scale = 1.0 / float(RANK * RANK * RANK_FOUR)
    total_rows = basis.shape[0]
    partial_gram = jnp.dot(
        regrouped, regrouped.T, precision=highest, preferred_element_type=jnp.float32
    )
    gram = lax.psum(partial_gram, ("wa", "an")) * factor_scale
    for step in range(ITERS):
        image = jnp.dot(gram, basis, precision=highest, preferred_element_type=jnp.float32)
        small = jnp.dot(image.T, image, precision=highest, preferred_element_type=jnp.float32)
        lower = jnp.linalg.cholesky(small)
        basis = lax.linalg.triangular_solve(
            lower, image, left_side=False, lower=True, transpose_a=True
        )
    out_rows = start_basis.shape[0]
    position = lax.axis_index("wa") * out_rows
    mine = lax.dynamic_slice_in_dim(basis, position, out_rows, 0)
    return mine * math.sqrt(total_rows)


def solution(mesh):
    in_specs = (P("wa", None, "an", None), P("wa", None), P("an", None), P(), P("wa", None))
    out_specs = P("wa", None)
    return jax.shard_map(
        per_device, mesh=mesh, in_specs=in_specs, out_specs=out_specs, check_vma=False
    )
```

profile of v0, /device:TPU:1, one launch (start us, length us, event | category | flops | bytes accessed | tf_op | source)
XLA Modules:
  0.0 424.3 jit_solution(207285124791887525)
XLA Ops:
  6.5 0.0 copy-start
  6.5 0.0 reduce-scatter.2.cloned.1.call-start
  6.5 26.5 %all_gather.6 = f32[1024,64]{1,0:T(8,128)S(1)} all-gather(f32[32,64]{1,0:T(8,128)} %param.9), channel_id=1, replica_groups=mesh['wa'=32,'an'=8] {'wa'}, dimensions={0}, use_global_device_ids=true | all-gather | bytes 270336 | tf_op jit(solution)/shard_map/all_gather | solution.py:16
  33.1 0.0 copy-done
  33.1 0.0 copy-start.2
  33.1 0.0 copy-start.4
  33.1 2.7 fusion.2
  35.8 0.0 copy-done.2
  35.8 1.8 convolution_bitcast_fusion
  37.6 0.0 copy-done.4
  37.6 2.5 fusion.5
  40.1 4.4 %copy.29 = f32[8,64,64,2]{0,3,2,1:T(2,128)} copy(f32[8,64,64,2]{2,3,1,0:T(2,128)S(1)} %fusion.5) | data formatting | bytes 524288 | tf_op jit(solution)/shard_map/aefd,dg->aefg/dot_general | solution.py:21
  44.6 0.0 copy-start.3
  44.6 0.0 reduce-scatter.2.cloned.1.call-update
  44.6 0.0 all-reduce.2.cloned.1.call-start
  44.7 55.8 %reduce-scatter.2.cloned.1.call-done = f32[8,1024]{0,1:T(8,128)} async-done(((f32[8,8192]{0,1:T(8,128)}), f32[8,1024]{0,1:T(8,128)}) %reduce-scatter.2.cloned.1.call-update) | async-done | bytes 32784 | tf_op jit(solution)/shard_map/reduce_scatter | solution.py:23
  100.5 1.2 copy.30
  101.7 0.1 reshape.35
  101.8 14.6 %all_to_all.19 = f32[32,1,256]{2,1,0:T(1,128)S(1)} all-to-all(f32[32,1,256]{2,1,0:T(1,128)S(1)} %reshape.35), channel_id=1, replica_groups=mesh['wa'=32,'an'=8] {'wa'}, dimensions={0} | all-to-all | bytes 65536 | tf_op jit(solution)/shard_map/all_to_all | solution.py:24
  116.4 0.5 broadcast.39
  116.9 0.7 reduce.4
  117.6 0.1 reshape.36
  117.7 1.1 fusion.16
  118.8 0.0 all-reduce.2.cloned.1.call-update
  118.8 0.0 copy-done.3
  118.8 23.1 %all_gather.7 = f32[256,64]{1,0:T(8,128)S(1)} all-gather(f32[8,64]{1,0:T(8,128)S(1)} %copy-done.3), channel_id=1, replica_groups=mesh['wa'=32,'an'=8] {'wa'}, dimensions={0}, use_global_device_ids=true | all-gather | bytes 67584 | tf_op jit(solution)/shard_map/all_gather | solution.py:17
  142.0 220.6 %all-reduce.2.cloned.1.call-done = f32[256,256]{1,0:T(8,128)} async-done(((f32[256,256]{1,0:T(8,128)}), f32[256,256]{1,0:T(8,128)}) %all-reduce.2.cloned.1.call-update) | async-done | bytes 262160 | tf_op jit(solution)/shard_map/psum | solution.py:30
  362.6 0.0 copy-start.1
  362.6 1.4 fusion.14
  364.0 0.2 fusion.47
  364.2 0.1 copy.31
  364.3 5.8 %cholesky.74 = f32[64,64]{1,0:T(8,128)S(1)} custom-call(f32[64,64]{1,0:T(8,128)S(1)} %fusion.33), custom_call_target="Cholesky" | custom-call | tf_op jit(solution)/shard_map/jit(cholesky)/cholesky | solution.py:34
  370.2 0.6 compare_reduce_fusion.3
  370.8 0.7 fusion.22
  371.5 4.9 %custom-call.8 = f32[1,64,64]{1,2,0:T(8,128)S(1)} custom-call(f32[1,64,64]{2,1,0:T(8,128)S(1)} %fusion.22), custom_call_target="InvertDiagBlocksLowerTriangular" | custom-call | tf_op jit(solution)/shard_map/triangular_solve/custom-call.0 | solution.py:35
  376.4 0.3 convolution_bitcast_fusion.4
  376.7 1.3 fusion.12
  378.0 0.2 fusion.48
  378.2 0.1 copy.32
  378.3 5.8 %cholesky.85 = f32[64,64]{1,0:T(8,128)S(1)} custom-call(f32[64,64]{1,0:T(8,128)S(1)} %fusion.31), custom_call_target="Cholesky" | custom-call | tf_op jit(solution)/shard_map/jit(cholesky)/cholesky | solution.py:34
  384.2 0.6 compare_reduce_fusion.2
  384.8 0.7 fusion.23
  385.5 4.9 %custom-call.9 = f32[1,64,64]{1,2,0:T(8,128)S(1)} custom-call(f32[1,64,64]{2,1,0:T(8,128)S(1)} %fusion.23), custom_call_target="InvertDiagBlocksLowerTriangular" | custom-call | tf_op jit(solution)/shard_map/triangular_solve/custom-call.0 | solution.py:35
  390.4 0.3 convolution_bitcast_fusion.3
  390.7 0.0 copy-done.1
  390.7 0.4 fusion.10
  391.0 0.2 fusion.49
  391.3 0.1 copy.33
  391.4 5.8 %cholesky.96 = f32[64,64]{1,0:T(8,128)S(1)} custom-call(f32[64,64]{1,0:T(8,128)S(1)} %fusion.29), custom_call_target="Cholesky" | custom-call | tf_op jit(solution)/shard_map/jit(cholesky)/cholesky | solution.py:34
  397.2 0.6 compare_reduce_fusion.1
  397.9 0.7 fusion.24
  398.5 4.9 %custom-call.10 = f32[1,64,64]{1,2,0:T(8,128)S(1)} custom-call(f32[1,64,64]{2,1,0:T(8,128)S(1)} %fusion.24), custom_call_target="InvertDiagBlocksLowerTriangular" | custom-call | tf_op jit(solution)/shard_map/triangular_solve/custom-call.0 | solution.py:35
  403.4 0.3 convolution_bitcast_fusion.2
  403.7 0.4 fusion.8
  404.1 0.2 fusion.50
  404.3 0.1 copy.34
  404.4 5.8 %cholesky.107 = f32[64,64]{1,0:T(8,128)S(1)} custom-call(f32[64,64]{1,0:T(8,128)S(1)} %fusion.27), custom_call_target="Cholesky" | custom-call | tf_op jit(solution)/shard_map/jit(cholesky)/cholesky | solution.py:34
  410.3 0.6 compare_reduce_fusion
  410.9 0.7 fusion.25
  411.6 4.9 %custom-call.11 = f32[1,64,64]{1,2,0:T(8,128)S(1)} custom-call(f32[1,64,64]{2,1,0:T(8,128)S(1)} %fusion.25), custom_call_target="InvertDiagBlocksLowerTriangular" | custom-call | tf_op jit(solution)/shard_map/triangular_solve/custom-call.0 | solution.py:35
  416.5 0.4 convolution_bitcast_fusion.1
  416.9 0.6 dynamic-slice_multiply_fusion
  (8 shorter events, 0.2 us)
Async XLA Ops:
  6.5 26.5 %copy-start = (f32[8,1024,16,4]{1,3,2,0:T(4,128)S(1)}, f32[8,1024,16,4]{1,3,2,0:T(4,128)}, u32[]{:S(2)}) copy-start(f32[8,1024,16,4]{1,3,2,0:T(4,128)} %param.8) | copy-start | bytes 6291460
  6.5 93.9 %reduce-scatter.2.cloned.1.call-start = ((), (), s32[]{:S(2)}) async-start(), calls=%async_computation.2 | async-start | bytes 4718592 | tf_op jit(solution)/shard_map/reduce_scatter | solution.py:23
  33.1 2.7 copy-start.2
  33.1 4.5 %copy-start.4 = (f32[4,2]{0,1:T(2,128)S(1)}, f32[4,2]{0,1:T(2,128)}, u32[]{:S(2)}) copy-start(f32[4,2]{0,1:T(2,128)} %param.11) | copy-start | bytes 100
  44.6 74.3 %copy-start.3 = (f32[8,64]{1,0:T(8,128)S(1)}, f32[8,64]{1,0:T(8,128)}, u32[]{:S(2)}) copy-start(f32[8,64]{1,0:T(8,128)} %param.12) | copy-start | bytes 6148
  44.6 318.0 %all-reduce.2.cloned.1.call-start = ((), (), s32[]{:S(2)}) async-start(), calls=%async_computation.3 | async-start | bytes 524288 | tf_op jit(solution)/shard_map/psum | solution.py:30
  362.6 28.1 %copy-start.1 = (f32[256,256]{1,0:T(8,128)S(1)}, f32[256,256]{1,0:T(8,128)}, u32[]{:S(2)}) copy-start(f32[256,256]{1,0:T(8,128)} %all-reduce.2.cloned.1.call-done) | copy-start | bytes 786436
Sparse Core Ops, SparseCore 0:
  44.7 55.7 reduce-scatter.1
  119.0 243.5 all-reduce.1
where the time goes:
time: 425 us; the launch traced here: 424 us
  waiting for transfers between devices  276 us (65%)
  blocking collectives  64.2 us (15%)
  other arithmetic  49.6 us (12%)
  between operations  13.7 us (3%)
  matrix products  13.6 us (3%)
  local copies, waits for them, and re-layouts  6.7 us (2%)
    psum x1, waiting for transfers between devices, per_device(): gram = lax.psum(partial_gram, ('wa', 'an')) * factor_scale  221 us
    reduce_scatter x1, waiting for transfers between devices, per_device(): shares = lax.psum_scatter(unfold, 'an', scatter_dimension=1, tiled=True)  55.8 us
    all_gather x1, blocking collectives, per_device(): lax.all_gather(factor_two, 'wa', axis=0, tiled=True)  26.5 us
    another operation x12, other arithmetic, per_device(): lower = jnp.linalg.cholesky(small)  26.1 us
    all_gather x1, blocking collectives, per_device(): lax.all_gather(start_basis, 'wa', axis=0, tiled=True)  23.1 us
    another operation x8, other arithmetic, per_device(): lax.linalg.triangular_solve(lower, image, left_side=False, lower=True, tr...  22.2 us
    all_to_all x1, blocking collectives, per_device(): lax.all_to_all(shares, 'wa', split_axis=1, concat_axis=0, tiled=True)  14.6 us
  transfers between devices with their start and end apart: 2, of which 2 were waited for; matrix products, arithmetic and copies ran while one was open for 0% of the time, Pallas kernels for 0%

commit v1 on v0

v1 whole, which is shorter than its diff:
```python
import functools
import math

import jax
import jax.numpy as jnp
from jax import lax
from jax.experimental import pallas as pl
from jax.experimental.pallas import tpu as pltpu
from jax.sharding import PartitionSpec as P

RANK = 64
RANK_FOUR = 2
ITERS = 4
NW, NZ = 32, 8
CHIPS = NW // 2
BLOCK = 8
MESH = pl.DeviceIdType.MESH
HIGHEST = lax.Precision.HIGHEST


def split3(x):
    h = x.astype(jnp.bfloat16)
    rest = x - h.astype(jnp.float32)
    m = rest.astype(jnp.bfloat16)
    l = (rest - m.astype(jnp.float32)).astype(jnp.bfloat16)
    return h, m, l


def mm(a, b, dims=((1,), (0,))):
    return lax.dot_general(
        a, b, (dims, ((), ())), precision=HIGHEST, preferred_element_type=jnp.float32
    )


def mm16(a, b):
    return jnp.dot(a, b, preferred_element_type=jnp.float32)


def lanes_of(tile, column):
    return jnp.broadcast_to(tile[:, column : column + 1], (8, 128))


def rows_of(tile, row):
    return jnp.broadcast_to(tile[row : row + 1, :], (8, 128))


def inverse_cholesky(w):
    row = lax.broadcasted_iota(jnp.int32, (8, 128), 0)
    lane = lax.broadcasted_iota(jnp.int32, (8, 128), 1)
    wide = jnp.concatenate([w, jnp.zeros((64, 64), jnp.float32)], axis=1)
    s = []
    for i in range(8):
        unit = jnp.where(lane == row + (64 + 8 * i), 1.0, 0.0)
        s.append(jnp.where(lane < 64, wide[8 * i : 8 * i + 8], unit))
    out = []
    for t in range(8):
        pivots = jnp.ones((8, 128), jnp.float32)
        for start in range(0, 8, BLOCK):
            cols = {
                i: [lanes_of(s[i], 8 * t + start + q) for q in range(BLOCK)]
                for i in range(t, 8)
            }
            for p in range(BLOCK):
                r = start + p
                pivot_row = rows_of(s[t], r)
                pivot = rows_of(cols[t][p], r)
                inverse = 1.0 / pivot
                heads = [rows_of(cols[t][q], r) for q in range(BLOCK)]
                for i in range(t, 8):
                    factor = cols[i][p] * inverse
                    if i == t:
                        factor = jnp.where(row > r, factor, 0.0)
                    s[i] = s[i] - factor * pivot_row
                    for q in range(p + 1, BLOCK):
                        cols[i][q] = cols[i][q] - factor * heads[q]
                pivots = jnp.where(row == r, pivot, pivots)
        out.append(s[t] * lax.rsqrt(pivots))
    return jnp.concatenate(out, axis=0)[:, 64:128]


def kernel(
    x_hbm, f2_hbm, f3_hbm, f4_hbm, b0_hbm, out_ref,
    xv, f2v, f3v, f4s, b0v, f2p, f2g, f3g, b0g, yh, ym, yl,
    s1, r1, vt, v_ref, a_ref, gp, g3, gsum, gfull, z_ref, linv_ref,
    loc, snd, rcv,
):
    w = lax.axis_index("wa")
    n = lax.axis_index("an")
    core = lax.rem(w, 2)
    chip = w // 2

    local = [
        pltpu.make_async_copy(f2_hbm, f2v, loc.at[0]),
        pltpu.make_async_copy(f3_hbm, f3v, loc.at[1]),
        pltpu.make_async_copy(b0_hbm, b0v, loc.at[2]),
        pltpu.make_async_copy(f4_hbm, f4s, loc.at[3]),
        pltpu.make_async_copy(x_hbm, xv, loc.at[4]),
    ]
    for copy in local:
        copy.start()

    barrier = pltpu.get_barrier_semaphore()

    def plane_peer(k):
        return lax.rem(w + k, NW), n

    def column_peer(k):
        return chip * 2 + lax.rem(core + k, 2), lax.rem(n + k // 2, NZ)

    @pl.loop(1, NW)
    def _(k):
        pl.semaphore_signal(barrier, inc=1, device_id=plane_peer(k), device_id_type=MESH)

    @pl.loop(2, 2 * NZ)
    def _(k):
        pl.semaphore_signal(barrier, inc=1, device_id=column_peer(k), device_id_type=MESH)

    local[0].wait()
    local[1].wait()
    local[2].wait()
    f2p[:, 0:64] = f2v[0:16, :]
    f2p[:, 64:128] = f2v[16:32, :]
    f2g[w] = f2p[...]
    f3g[n] = f3v[...]
    b0g[w] = b0v[...]

    pl.semaphore_wait(barrier, NW - 1 + 2 * NZ - 2)

    def send(stage, src, dst, peer):
        pltpu.make_async_remote_copy(
            src_ref=src, dst_ref=dst, send_sem=snd.at[stage], recv_sem=rcv.at[stage],
            device_id=peer, device_id_type=MESH,
        ).start()

    def await_all(sem, blocks):
        pltpu.make_async_copy(blocks, blocks, sem).wait()

    @pl.loop(1, NW)
    def _(k):
        send(0, f2p, f2g.at[w], plane_peer(k))

    @pl.loop(1, NZ)
    def _(k):
        send(1, f3v, f3g.at[n], (w, lax.rem(n + k, NZ)))

    @pl.loop(1, NW)
    def _(k):
        send(2, b0v, b0g.at[w], plane_peer(k))

    local[3].wait()
    local[4].wait()
    for bt in range(8):
        parts = [xv[pl.ds(bt * 4 + d, 128, stride=32), :] for d in range(4)]
        for g in range(2):
            total = parts[0] * f4s[g, 0]
            for d in range(1, 4):
                total = total + parts[d] * f4s[g, d]
            h, m, l = split3(total)
            here = (slice(128 * g, 128 * g + 128), slice(128 * bt, 128 * bt + 128))
            yh[here] = h
            ym[here] = m
            yl[here] = l

    await_all(rcv.at[0], f2g.at[pl.ds(0, NW - 1)])
    packed = f2g[...]
    full_two = jnp.concatenate([packed[:, :, 0:64], packed[:, :, 64:128]], axis=1)
    wh, wm, wl = split3(full_two.reshape(1024, 64))
    p0 = mm16(yh[...], jnp.concatenate([wh, wm, wl], axis=1))
    p1 = mm16(ym[...], jnp.concatenate([wh, wm], axis=1))
    p2 = mm16(yl[...], wh)
    first = (p0[:, 128:192] + p1[:, 64:128] + p2) + (p0[:, 64:128] + p1[:, 0:64]) + p0[:, 0:64]
    for g in range(2):
        s1[g] = first[128 * g : 128 * g + 128].T.reshape(8, 8, 128)

    @pl.loop(1, 2 * NZ)
    def _(k):
        to_w, to_n = column_peer(k)
        send(3, s1.at[lax.rem(to_w, 2), to_n], r1.at[core * NZ + n], (to_w, to_n))

    r1[core * NZ + n] = s1[core, n]
    await_all(rcv.at[1], f3g.at[pl.ds(0, NZ - 1)])
    full_three = f3g[...].reshape(128, 64)
    await_all(rcv.at[3], r1.at[pl.ds(0, 2 * NZ - 1)])

    lane = lax.broadcasted_iota(jnp.int32, (8, 128), 1)
    rows = []
    for s in range(2):
        v = [r1[s * NZ + m] for m in range(NZ)]
        for d in (4, 2, 1):
            upper = lax.rem(lane // (16 * d), 2) == 1
            nxt = list(v)
            for i in range(8):
                if i & d == 0:
                    j = i + d
                    nxt[i] = jnp.where(upper, pltpu.roll(v[j], 16 * d, 1), v[i])
                    nxt[j] = jnp.where(upper, v[j], pltpu.roll(v[i], 128 - 16 * d, 1))
            v = nxt
        rows += v
    vt[...] = mm(jnp.concatenate(rows, axis=0), full_three)
    for e in range(8):
        v_ref[:, 64 * e : 64 * e + 64] = vt[pl.ds(e, 16, stride=8), :]

    @pl.loop(1, CHIPS)
    def _(k):
        send(4, v_ref, a_ref.at[chip], (lax.rem(chip + k, CHIPS) * 2 + core, n))

    a_ref[chip] = v_ref[...]
    await_all(rcv.at[4], a_ref.at[pl.ds(0, CHIPS - 1)])
    partial = mm(v_ref[...], a_ref[...].reshape(256, 512), ((1,), (1,)))
    gp[...] = partial.reshape(2, 8, 256)

    @pl.loop(1, 2 * NZ)
    def _(k):
        to_w, to_n = column_peer(k)
        send(5, gp.at[lax.rem(to_w, 2)], g3.at[core * NZ + n], (to_w, to_n))

    g3[core * NZ + n] = gp[core]
    await_all(rcv.at[5], g3.at[pl.ds(0, 2 * NZ - 1)])
    total = g3[0]
    for i in range(1, 2 * NZ):
        total = total + g3[i]
    gsum[...] = total * (1.0 / float(RANK * RANK * RANK_FOUR))

    @pl.loop(1, NW)
    def _(k):
        send(6, gsum, gfull.at[w], plane_peer(k))

    gfull[w] = gsum[...]
    await_all(rcv.at[2], b0g.at[pl.ds(0, NW - 1)])
    basis = b0g[...].reshape(256, 64)
    await_all(rcv.at[6], gfull.at[pl.ds(0, NW - 1)])

    z_ref[...] = mm(gfull[...].reshape(256, 256), basis)

    @pl.loop(0, ITERS)
    def _(step):
        z = z_ref[...]
        linv_ref[...] = inverse_cholesky(mm(z, z, ((0,), (0,))))

        @pl.when(step < ITERS - 1)
        def _():
            image = mm(gfull[...].reshape(256, 256), z)
            z_ref[...] = mm(image, linv_ref[...], ((1,), (1,)))

    mine = z_ref[pl.ds(pl.multiple_of(w * 8, 8), 8), :]
    out_ref[...] = mm(mine, linv_ref[...], ((1,), (1,))) * math.sqrt(256.0)

    await_all(snd.at[0], f2g.at[pl.ds(0, NW - 1)])
    await_all(snd.at[1], f3g.at[pl.ds(0, NZ - 1)])
    await_all(snd.at[2], b0g.at[pl.ds(0, NW - 1)])
    await_all(snd.at[3], r1.at[pl.ds(0, 2 * NZ - 1)])
    await_all(snd.at[4], a_ref.at[pl.ds(0, CHIPS - 1)])
    await_all(snd.at[5], g3.at[pl.ds(0, 2 * NZ - 1)])
    await_all(snd.at[6], gfull.at[pl.ds(0, NW - 1)])


def per_device(tensor, factor_two, factor_three, factor_four, start_basis):
    f32, bf16 = jnp.float32, jnp.bfloat16
    x = tensor.reshape(8, 8, 128, 16, 4).transpose(0, 3, 1, 4, 2).reshape(4096, 128)
    hbm = pl.BlockSpec(memory_space=pltpu.HBM)
    return pl.pallas_call(
        kernel,
        out_shape=jax.ShapeDtypeStruct((8, 64), f32),
        in_specs=[hbm] * 5,
        out_specs=pl.BlockSpec(memory_space=pltpu.VMEM),
        scratch_shapes=[
            pltpu.VMEM((4096, 128), f32),
            pltpu.VMEM((32, 64), f32),
            pltpu.VMEM((16, 64), f32),
            pltpu.SMEM((2, 4), f32),
            pltpu.VMEM((8, 64), f32),
            pltpu.VMEM((16, 128), f32),
            pltpu.VMEM((NW, 16, 128), f32),
            pltpu.VMEM((NZ, 16, 64), f32),
            pltpu.VMEM((NW, 8, 64), f32),
            pltpu.VMEM((256, 1024), bf16),
            pltpu.VMEM((256, 1024), bf16),
            pltpu.VMEM((256, 1024), bf16),
            pltpu.VMEM((2, 8, 8, 128), f32),
            pltpu.VMEM((16, 8, 128), f32),
            pltpu.VMEM((128, 64), f32),
            pltpu.VMEM((16, 512), f32),
            pltpu.VMEM((CHIPS, 16, 512), f32),
            pltpu.VMEM((2, 8, 256), f32),
            pltpu.VMEM((16, 8, 256), f32),
            pltpu.VMEM((8, 256), f32),
            pltpu.VMEM((NW, 8, 256), f32),
            pltpu.VMEM((256, 64), f32),
            pltpu.VMEM((64, 64), f32),
            pltpu.SemaphoreType.DMA((5,)),
            pltpu.SemaphoreType.DMA((7,)),
            pltpu.SemaphoreType.DMA((7,)),
        ],
        compiler_params=pltpu.CompilerParams(
            collective_id=0, has_side_effects=True, vmem_limit_bytes=40 * 2**20
        ),
        name="hooi",
    )(x, factor_two, factor_three, factor_four.T, start_basis)


def solution(mesh):
    in_specs = (P("wa", None, "an", None), P("wa", None), P("an", None), P(), P("wa", None))
    return jax.shard_map(
        per_device, mesh=mesh, in_specs=in_specs, out_specs=P("wa", None), check_vma=False
    )
```

time: 425 us -> 63.9 us (0.15)
  waiting for transfers between devices: 276 us -> 0 us
  blocking collectives: 64.2 us -> 0 us
  Pallas kernels: 0 us -> 58.6 us
  other arithmetic: 49.6 us -> 0 us
  between operations: 13.7 us -> 0.01 us
  matrix products: 13.6 us -> 0 us
    psum x1 -> x0, waiting for transfers between devices: 221 us -> none  [per_device(): gram = lax.psum(partial_gram, ('wa', 'an')) * factor_scale]
    pallas_call x0 -> x1, Pallas kernels: none -> 58.6 us  [per_device(): pl.pallas_call(kernel, out_shape=jax.ShapeDtypeStruct((8, 64), f32), in_s...]
    reduce_scatter x1 -> x0, waiting for transfers between devices: 55.8 us -> none  [per_device(): shares = lax.psum_scatter(unfold, 'an', scatter_dimension=1, tiled=True)]
    all_gather x2 -> x0, blocking collectives: 49.7 us -> none  [the longest x1 26.5 us: per_device(): lax.all_gather(factor_two, 'wa', axis=0, tiled=True)]
    another operation x20 -> x0, other arithmetic: 48.3 us -> none  [the longest x12 26.1 us: per_device(): lower = jnp.linalg.cholesky(small)]
    all_to_all x1 -> x0, blocking collectives: 14.6 us -> none  [per_device(): lax.all_to_all(shares, 'wa', split_axis=1, concat_axis=0, tiled=True)]
    dot_general x12 -> x0, matrix products: 12.4 us -> none  [the longest x4 3.47 us: per_device(): jnp.dot(gram, basis, precision=highest, preferred_element_type=jnp.float32)]
    dot_general x5 -> x0, local copies, waits for them, and re-layouts: 4.74 us -> none  [the longest x1 4.44 us: per_device(): core = jnp.einsum('aefd,dg->aefg', second, factor_four, precision=highest)]
  transfers between devices with their start and end apart: 2 -> 0, of which waited for: 2 -> 0; matrix products, arithmetic and copies ran while one was open for 0% -> 0% of each run, Pallas kernels for 0% -> 0%
where the time goes in v1:
time: 63.9 us; the launch traced here: 63.6 us
  Pallas kernels  58.6 us (92%)
  local copies, waits for them, and re-layouts  4.96 us (8%)
    pallas_call x1, Pallas kernels, per_device(): pl.pallas_call(kernel, out_shape=jax.ShapeDtypeStruct((8, 64), f32), in_s...  58.6 us
    unnamed x11, local copies, waits for them, and re-layouts  4.96 us

profile of v1, /device:TPU:1, one launch (start us, length us, event | category | flops | bytes accessed | tf_op | source)
XLA Modules:
  0.0 63.6 jit_solution(4646019599771578416)
XLA Ops:
  0.0 0.0 copy-start
  0.0 1.6 %copy-done = f32[8,1024,16,4]{1,3,2,0:T(4,128)S(1)} copy-done((f32[8,1024,16,4]{1,3,2,0:T(4,128)S(1)}, f32[8,1024,16,4]{1,3,2,0:T(4,128)}, u32[]{:S(2)}) %copy-start) | copy-done | bytes 2097176
  1.6 0.0 copy-start.1
  1.6 0.7 %copy-done.1 = f32[32,64]{1,0:T(8,128)S(1)} copy-done((f32[32,64]{1,0:T(8,128)S(1)}, f32[32,64]{1,0:T(8,128)}, u32[]{:S(2)}) %copy-start.1) | copy-done | bytes 8216
  2.3 0.0 copy-start.2
  2.3 0.7 %copy-done.2 = f32[16,64]{1,0:T(8,128)S(1)} copy-done((f32[16,64]{1,0:T(8,128)S(1)}, f32[16,64]{1,0:T(8,128)}, u32[]{:S(2)}) %copy-start.2) | copy-done | bytes 4120
  3.0 0.0 copy-start.3
  3.0 0.7 %copy-done.3 = f32[8,64]{1,0:T(8,128)S(1)} copy-done((f32[8,64]{1,0:T(8,128)S(1)}, f32[8,64]{1,0:T(8,128)}, u32[]{:S(2)}) %copy-start.3) | copy-done | bytes 2072
  3.7 0.0 copy-start.4
  3.7 0.7 %copy-done.4 = f32[4,2]{0,1:T(2,128)S(1)} copy-done((f32[4,2]{0,1:T(2,128)S(1)}, f32[4,2]{0,1:T(2,128)}, u32[]{:S(2)}) %copy-start.4) | copy-done | bytes 56
  4.4 58.6 %hooi.1 = f32[8,64]{1,0:T(8,128)S(1)} custom-call(f32[4096,128]{1,0:T(8,128)S(1)} %bitcast.6, f32[32,64]{1,0:T(8,128)S(1)} %copy-done.1, f32[16,64]{1,0:T(8,128)S(1)} %copy-done.2, f32[2,4]{1,0:T(2,128)S(1)} %bitcast.7, f32[8,64]{1,0:T(8,128)S(1)} %copy-done.3), custom_call_target="tpu_custom_call" | custom-call | tf_op jit(solution)/shard_map/hooi/pallas_call | solution.py:261
  63.0 0.6 copy.8
Async XLA Ops:
  0.0 1.6 %copy-start = (f32[8,1024,16,4]{1,3,2,0:T(4,128)S(1)}, f32[8,1024,16,4]{1,3,2,0:T(4,128)}, u32[]{:S(2)}) copy-start(f32[8,1024,16,4]{1,3,2,0:T(4,128)} %param.5) | copy-start | bytes 6291460
  1.6 0.7 %copy-start.1 = (f32[32,64]{1,0:T(8,128)S(1)}, f32[32,64]{1,0:T(8,128)}, u32[]{:S(2)}) copy-start(f32[32,64]{1,0:T(8,128)} %f2_hbm.1) | copy-start | bytes 24580
  2.3 0.7 %copy-start.2 = (f32[16,64]{1,0:T(8,128)S(1)}, f32[16,64]{1,0:T(8,128)}, u32[]{:S(2)}) copy-start(f32[16,64]{1,0:T(8,128)} %f3_hbm.1) | copy-start | bytes 12292
  3.0 0.7 %copy-start.3 = (f32[8,64]{1,0:T(8,128)S(1)}, f32[8,64]{1,0:T(8,128)}, u32[]{:S(2)}) copy-start(f32[8,64]{1,0:T(8,128)} %b0_hbm.1) | copy-start | bytes 6148
  3.7 0.7 %copy-start.4 = (f32[4,2]{0,1:T(2,128)S(1)}, f32[4,2]{0,1:T(2,128)}, u32[]{:S(2)}) copy-start(f32[4,2]{0,1:T(2,128)} %param.8) | copy-start | bytes 100

commit v2 on v1

--- a/solution.py
+++ b/solution.py
@@ -124,29 +124,6 @@
     f3g[n] = f3v[...]
     b0g[w] = b0v[...]
 
-    pl.semaphore_wait(barrier, NW - 1 + 2 * NZ - 2)
-
-    def send(stage, src, dst, peer):
-        pltpu.make_async_remote_copy(
-            src_ref=src, dst_ref=dst, send_sem=snd.at[stage], recv_sem=rcv.at[stage],
-            device_id=peer, device_id_type=MESH,
-        ).start()
-
-    def await_all(sem, blocks):
-        pltpu.make_async_copy(blocks, blocks, sem).wait()
-
-    @pl.loop(1, NW)
-    def _(k):
-        send(0, f2p, f2g.at[w], plane_peer(k))
-
-    @pl.loop(1, NZ)
-    def _(k):
-        send(1, f3v, f3g.at[n], (w, lax.rem(n + k, NZ)))
-
-    @pl.loop(1, NW)
-    def _(k):
-        send(2, b0v, b0g.at[w], plane_peer(k))
-
     local[3].wait()
     local[4].wait()
     for bt in range(8):
@@ -161,6 +138,25 @@
             ym[here] = m
             yl[here] = l
 
+    pl.semaphore_wait(barrier, NW - 1 + 2 * NZ - 2)
+
+    def send(stage, src, dst, peer):
+        pltpu.make_async_remote_copy(
+            src_ref=src, dst_ref=dst, send_sem=snd.at[stage], recv_sem=rcv.at[stage],
+            device_id=peer, device_id_type=MESH,
+        ).start()
+
+    def await_all(sem, blocks):
+        pltpu.make_async_copy(blocks, blocks, sem).wait()
+
+    @pl.loop(1, NW)
+    def _(k):
+        send(0, f2p, f2g.at[w], plane_peer(k))
+
+    @pl.loop(1, NZ)
+    def _(k):
+        send(1, f3v, f3g.at[n], (w, lax.rem(n + k, NZ)))
+
     await_all(rcv.at[0], f2g.at[pl.ds(0, NW - 1)])
     packed = f2g[...]
     full_two = jnp.concatenate([packed[:, :, 0:64], packed[:, :, 64:128]], axis=1)
@@ -176,6 +172,10 @@
     def _(k):
         to_w, to_n = column_peer(k)
         send(3, s1.at[lax.rem(to_w, 2), to_n], r1.at[core * NZ + n], (to_w, to_n))
+
+    @pl.loop(1, NW)
+    def _(k):
+        send(2, b0v, b0g.at[w], plane_peer(k))
 
     r1[core * NZ + n] = s1[core, n]
     await_all(rcv.at[1], f3g.at[pl.ds(0, NZ - 1)])
@@ -292,7 +292,7 @@
             pltpu.SemaphoreType.DMA((7,)),
         ],
         compiler_params=pltpu.CompilerParams(
-            collective_id=0, has_side_effects=True, vmem_limit_bytes=40 * 2**20
+            collective_id=0, has_side_effects=True, vmem_limit_bytes=60 * 2**20
         ),
         name="hooi",
     )(x, factor_two, factor_three, factor_four.T, start_basis)

time: 63.9 us -> 59.7 us (0.934)
  local copies, waits for them, and re-layouts: 4.96 us -> 1.28 us
    unnamed x11 -> x1, local copies, waits for them, and re-layouts: 4.96 us -> 1.28 us
where the time goes in v2:
time: 59.7 us; the launch traced here: 59.5 us
  Pallas kernels  58.2 us (97%)
  local copies, waits for them, and re-layouts  1.28 us (2%)
    pallas_call x1, Pallas kernels, per_device(): pl.pallas_call(kernel, out_shape=jax.ShapeDtypeStruct((8, 64), f32), in_s...  58.2 us
    unnamed x1, local copies, waits for them, and re-layouts  1.28 us

profile of v2, /device:TPU:1, one launch (start us, length us, event | category | flops | bytes accessed | tf_op | source)
XLA Modules:
  0.0 59.5 jit_solution(16335506212843799136)
XLA Ops:
  0.0 58.2 %hooi.1 = f32[8,64]{1,0:T(8,128)} custom-call(f32[4096,128]{1,0:T(8,128)} %bitcast.6, f32[32,64]{1,0:T(8,128)} %f2_hbm.1, f32[16,64]{1,0:T(8,128)} %f3_hbm.1, f32[2,4]{1,0:T(2,128)} %bitcast.7, f32[8,64]{1,0:T(8,128)} %b0_hbm.1), custom_call_target="tpu_custom_call" | custom-call | tf_op jit(solution)/shard_map/hooi/pallas_call | solution.py:261
  58.2 1.3 %copy.8 = f32[8,64]{1,0:T(8,128)} copy(f32[8,64]{1,0:T(8,128)} %hooi.1) | data formatting | bytes 4096

commit v3 on v2

--- a/solution.py
+++ b/solution.py
@@ -13,6 +13,7 @@
 ITERS = 4
 NW, NZ = 32, 8
 CHIPS = NW // 2
+HALF = CHIPS // 2
 BLOCK = 8
 MESH = pl.DeviceIdType.MESH
 HIGHEST = lax.Precision.HIGHEST
@@ -81,13 +82,15 @@
 def kernel(
     x_hbm, f2_hbm, f3_hbm, f4_hbm, b0_hbm, out_ref,
     xv, f2v, f3v, f4s, b0v, f2p, f2g, f3g, b0g, yh, ym, yl,
-    s1, r1, vt, v_ref, a_ref, gp, g3, gsum, gfull, z_ref, linv_ref,
+    s1, r1, vt, v_ref, a_ref, gp, g3, gsum, gfull, gmat, z_ref, linv_ref,
     loc, snd, rcv,
 ):
     w = lax.axis_index("wa")
     n = lax.axis_index("an")
     core = lax.rem(w, 2)
     chip = w // 2
+    label = lax.rem(7 * chip, CHIPS)
+    slot = label * 2 + core
 
     local = [
         pltpu.make_async_copy(f2_hbm, f2v, loc.at[0]),
@@ -122,7 +125,7 @@
     f2p[:, 64:128] = f2v[16:32, :]
     f2g[w] = f2p[...]
     f3g[n] = f3v[...]
-    b0g[w] = b0v[...]
+    b0g[slot] = b0v[...]
 
     local[3].wait()
     local[4].wait()
@@ -175,7 +178,7 @@
 
     @pl.loop(1, NW)
     def _(k):
-        send(2, b0v, b0g.at[w], plane_peer(k))
+        send(2, b0v, b0g.at[slot], plane_peer(k))
 
     r1[core * NZ + n] = s1[core, n]
     await_all(rcv.at[1], f3g.at[pl.ds(0, NZ - 1)])
@@ -200,37 +203,66 @@
     for e in range(8):
         v_ref[:, 64 * e : 64 * e + 64] = vt[pl.ds(e, 16, stride=8), :]
 
-    @pl.loop(1, CHIPS)
-    def _(k):
-        send(4, v_ref, a_ref.at[chip], (lax.rem(chip + k, CHIPS) * 2 + core, n))
-
-    a_ref[chip] = v_ref[...]
-    await_all(rcv.at[4], a_ref.at[pl.ds(0, CHIPS - 1)])
-    partial = mm(v_ref[...], a_ref[...].reshape(256, 512), ((1,), (1,)))
-    gp[...] = partial.reshape(2, 8, 256)
+    @pl.loop(1, HALF + 1)
+    def _(k):
+        to = lax.rem(7 * lax.rem(label + CHIPS - k, CHIPS), CHIPS)
+        send(4, v_ref, a_ref.at[k], (to * 2 + core, n))
+
+    a_ref[0] = v_ref[...]
+    await_all(rcv.at[4], a_ref.at[pl.ds(1, HALF)])
+    partial = mm(v_ref[...], a_ref[...].reshape(144, 512), ((1,), (1,)))
+    row = lax.broadcasted_iota(jnp.int32, (8, 128), 0)
+    for s in range(2):
+        gp[s, 0:8] = partial[8 * s : 8 * s + 8, 0:128]
+        last = jnp.concatenate([partial[8 * s : 8 * s + 8, 128:144]] * 8, axis=1)
+        gp[s, 8:9] = jnp.sum(jnp.where(lane // 16 == lax.rem(8 - row, 8), last, 0.0), axis=0, keepdims=True)
 
     @pl.loop(1, 2 * NZ)
     def _(k):
         to_w, to_n = column_peer(k)
-        send(5, gp.at[lax.rem(to_w, 2)], g3.at[core * NZ + n], (to_w, to_n))
-
-    g3[core * NZ + n] = gp[core]
-    await_all(rcv.at[5], g3.at[pl.ds(0, 2 * NZ - 1)])
-    total = g3[0]
-    for i in range(1, 2 * NZ):
-        total = total + g3[i]
-    gsum[...] = total * (1.0 / float(RANK * RANK * RANK_FOUR))
+        send(
+            5, gp.at[lax.rem(to_w, 2), pl.ds(0, 9)], g3.at[core * NZ + n, pl.ds(0, 9)], (to_w, to_n)
+        )
+
+    g3[core * NZ + n, 0:9] = gp[core, 0:9]
+    await_all(rcv.at[5], g3.at[pl.ds(0, 2 * NZ - 1), pl.ds(0, 9)])
+    for part in (slice(0, 8), slice(8, 9)):
+        total = g3[0, part]
+        for i in range(1, 2 * NZ):
+            total = total + g3[i, part]
+        gsum[part] = total * (1.0 / float(RANK * RANK * RANK_FOUR))
 
     @pl.loop(1, NW)
     def _(k):
-        send(6, gsum, gfull.at[w], plane_peer(k))
-
-    gfull[w] = gsum[...]
+        send(6, gsum.at[pl.ds(0, 9)], gfull.at[slot, pl.ds(0, 9)], plane_peer(k))
+
+    gfull[slot, 0:9] = gsum[0:9]
     await_all(rcv.at[2], b0g.at[pl.ds(0, NW - 1)])
     basis = b0g[...].reshape(256, 64)
-    await_all(rcv.at[6], gfull.at[pl.ds(0, NW - 1)])
-
-    z_ref[...] = mm(gfull[...].reshape(256, 256), basis)
+    await_all(rcv.at[6], gfull.at[pl.ds(0, NW - 1), pl.ds(0, 9)])
+
+    for i in range(CHIPS):
+        at = 16 * (i % 8)
+        for c in range(2):
+            body = gfull[2 * i + c, 0:8]
+            if at:
+                body = pltpu.roll(body, at, 1)
+            last = jnp.broadcast_to(gfull[2 * i + c, 8:9], (8, 128))
+            last = pltpu.roll(last, 0, 1, stride=16, stride_axis=0)
+            if at:
+                last = pltpu.roll(last, at, 1)
+            near = jnp.where(lane >= at, body, 0.0)
+            far = jnp.where(lane < at, body, jnp.where(lane < at + 16, last, 0.0))
+            half = i // 8
+            rows = slice(16 * i + 8 * c, 16 * i + 8 * c + 8)
+            gmat[rows, 128 * half : 128 * half + 128] = near
+            gmat[rows, 128 - 128 * half : 256 - 128 * half] = far
+    half_gram = gmat[...]
+    row_block = lax.broadcasted_iota(jnp.int32, (256, 256), 0) // 16
+    column_block = lax.broadcasted_iota(jnp.int32, (256, 256), 1) // 16
+    held = lax.rem(column_block - row_block + CHIPS, CHIPS) <= HALF
+    gmat[...] = jnp.where(held, half_gram, half_gram.T)
+    z_ref[...] = mm(gmat[...], basis)
 
     @pl.loop(0, ITERS)
     def _(step):
@@ -239,19 +271,19 @@
 
         @pl.when(step < ITERS - 1)
         def _():
-            image = mm(gfull[...].reshape(256, 256), z)
+            image = mm(gmat[...], z)
             z_ref[...] = mm(image, linv_ref[...], ((1,), (1,)))
 
-    mine = z_ref[pl.ds(pl.multiple_of(w * 8, 8), 8), :]
+    mine = z_ref[pl.ds(pl.multiple_of(slot * 8, 8), 8), :]
     out_ref[...] = mm(mine, linv_ref[...], ((1,), (1,))) * math.sqrt(256.0)
 
     await_all(snd.at[0], f2g.at[pl.ds(0, NW - 1)])
     await_all(snd.at[1], f3g.at[pl.ds(0, NZ - 1)])
     await_all(snd.at[2], b0g.at[pl.ds(0, NW - 1)])
     await_all(snd.at[3], r1.at[pl.ds(0, 2 * NZ - 1)])
-    await_all(snd.at[4], a_ref.at[pl.ds(0, CHIPS - 1)])
-    await_all(snd.at[5], g3.at[pl.ds(0, 2 * NZ - 1)])
-    await_all(snd.at[6], gfull.at[pl.ds(0, NW - 1)])
+    await_all(snd.at[4], a_ref.at[pl.ds(1, HALF)])
+    await_all(snd.at[5], g3.at[pl.ds(0, 2 * NZ - 1), pl.ds(0, 9)])
+    await_all(snd.at[6], gfull.at[pl.ds(0, NW - 1), pl.ds(0, 9)])
 
 
 def per_device(tensor, factor_two, factor_three, factor_four, start_basis):
@@ -280,11 +312,12 @@
             pltpu.VMEM((16, 8, 128), f32),
             pltpu.VMEM((128, 64), f32),
             pltpu.VMEM((16, 512), f32),
-            pltpu.VMEM((CHIPS, 16, 512), f32),
-            pltpu.VMEM((2, 8, 256), f32),
-            pltpu.VMEM((16, 8, 256), f32),
-            pltpu.VMEM((8, 256), f32),
-            pltpu.VMEM((NW, 8, 256), f32),
+            pltpu.VMEM((HALF + 1, 16, 512), f32),
+            pltpu.VMEM((2, 16, 128), f32),
+            pltpu.VMEM((16, 16, 128), f32),
+            pltpu.VMEM((16, 128), f32),
+            pltpu.VMEM((NW, 16, 128), f32),
+            pltpu.VMEM((256, 256), f32),
             pltpu.VMEM((256, 64), f32),
             pltpu.VMEM((64, 64), f32),
             pltpu.SemaphoreType.DMA((5,)),

time: 59.7 us -> 55 us (0.921)
  Pallas kernels: 58.2 us -> 53.6 us
    pallas_call x1, Pallas kernels: 58.2 us -> 53.6 us  [per_device(): pl.pallas_call(kernel, out_shape=jax.ShapeDtypeStruct((8, 64), f32), in_s...]
where the time goes in v3:
time: 55 us; the launch traced here: 54.9 us
  Pallas kernels  53.6 us (97%)
  local copies, waits for them, and re-layouts  1.28 us (2%)
    pallas_call x1, Pallas kernels, per_device(): pl.pallas_call(kernel, out_shape=jax.ShapeDtypeStruct((8, 64), f32), in_s...  53.6 us
    unnamed x1, local copies, waits for them, and re-layouts  1.28 us

profile of v3, /device:TPU:1, one launch (start us, length us, event | category | flops | bytes accessed | tf_op | source)
XLA Modules:
  0.0 54.9 jit_solution(901474460329056378)
XLA Ops:
  0.0 53.6 %hooi.1 = f32[8,64]{1,0:T(8,128)} custom-call(f32[4096,128]{1,0:T(8,128)} %bitcast.6, f32[32,64]{1,0:T(8,128)} %f2_hbm.1, f32[16,64]{1,0:T(8,128)} %f3_hbm.1, f32[2,4]{1,0:T(2,128)} %bitcast.7, f32[8,64]{1,0:T(8,128)} %b0_hbm.1), custom_call_target="tpu_custom_call" | custom-call | tf_op jit(solution)/shard_map/hooi/pallas_call | solution.py:293
  53.6 1.3 %copy.8 = f32[8,64]{1,0:T(8,128)} copy(f32[8,64]{1,0:T(8,128)} %hooi.1) | data formatting | bytes 4096

commit v4 on v3

--- a/solution.py
+++ b/solution.py
@@ -15,6 +15,10 @@
 CHIPS = NW // 2
 HALF = CHIPS // 2
 BLOCK = 8
+PLANE = sorted(
+    [(x, y, c) for x in range(4) for y in range(4) for c in range(2) if x or y or c],
+    key=lambda p: -(min(p[0], 4 - p[0]) + min(p[1], 4 - p[1])),
+)
 MESH = pl.DeviceIdType.MESH
 HIGHEST = lax.Precision.HIGHEST
 
@@ -104,17 +108,21 @@
 
     barrier = pltpu.get_barrier_semaphore()
 
-    def plane_peer(k):
-        return lax.rem(w + k, NW), n
+    def plane_peers():
+        for dx, dy, dc in PLANE:
+            to = lax.rem(chip // 4 + dx, 4) * 4 + lax.rem(chip + dy, 4)
+            yield to * 2 + lax.rem(core + dc, 2), n
 
     def column_peer(k):
-        return chip * 2 + lax.rem(core + k, 2), lax.rem(n + k // 2, NZ)
-
-    @pl.loop(1, NW)
-    def _(k):
-        pl.semaphore_signal(barrier, inc=1, device_id=plane_peer(k), device_id_type=MESH)
-
-    @pl.loop(2, 2 * NZ)
+        step = k // 2
+        reach = (step + 1) // 2
+        dz = NZ // 2 + reach * (1 - 2 * lax.rem(step, 2))
+        return chip * 2 + lax.rem(core + k + 1, 2), lax.rem(n + dz, NZ)
+
+    for peer in plane_peers():
+        pl.semaphore_signal(barrier, inc=1, device_id=peer, device_id_type=MESH)
+
+    @pl.loop(0, 2 * NZ - 2)
     def _(k):
         pl.semaphore_signal(barrier, inc=1, device_id=column_peer(k), device_id_type=MESH)
 
@@ -126,6 +134,24 @@
     f2g[w] = f2p[...]
     f3g[n] = f3v[...]
     b0g[slot] = b0v[...]
+
+    pl.semaphore_wait(barrier, NW - 1 + 2 * NZ - 2)
+
+    def send(stage, src, dst, peer):
+        pltpu.make_async_remote_copy(
+            src_ref=src, dst_ref=dst, send_sem=snd.at[stage], recv_sem=rcv.at[stage],
+            device_id=peer, device_id_type=MESH,
+        ).start()
+
+    def await_all(sem, blocks):
+        pltpu.make_async_copy(blocks, blocks, sem).wait()
+
+    for peer in plane_peers():
+        send(0, f2p, f2g.at[w], peer)
+
+    @pl.loop(1, NZ)
+    def _(k):
+        send(1, f3v, f3g.at[n], (w, lax.rem(n + k, NZ)))
 
     local[3].wait()
     local[4].wait()
@@ -141,25 +167,6 @@
             ym[here] = m
             yl[here] = l
 
-    pl.semaphore_wait(barrier, NW - 1 + 2 * NZ - 2)
-
-    def send(stage, src, dst, peer):
-        pltpu.make_async_remote_copy(
-            src_ref=src, dst_ref=dst, send_sem=snd.at[stage], recv_sem=rcv.at[stage],
-            device_id=peer, device_id_type=MESH,
-        ).start()
-
-    def await_all(sem, blocks):
-        pltpu.make_async_copy(blocks, blocks, sem).wait()
-
-    @pl.loop(1, NW)
-    def _(k):
-        send(0, f2p, f2g.at[w], plane_peer(k))
-
-    @pl.loop(1, NZ)
-    def _(k):
-        send(1, f3v, f3g.at[n], (w, lax.rem(n + k, NZ)))
-
     await_all(rcv.at[0], f2g.at[pl.ds(0, NW - 1)])
     packed = f2g[...]
     full_two = jnp.concatenate([packed[:, :, 0:64], packed[:, :, 64:128]], axis=1)
@@ -171,14 +178,13 @@
     for g in range(2):
         s1[g] = first[128 * g : 128 * g + 128].T.reshape(8, 8, 128)
 
-    @pl.loop(1, 2 * NZ)
+    @pl.loop(0, 2 * NZ - 1)
     def _(k):
         to_w, to_n = column_peer(k)
         send(3, s1.at[lax.rem(to_w, 2), to_n], r1.at[core * NZ + n], (to_w, to_n))
 
-    @pl.loop(1, NW)
-    def _(k):
-        send(2, b0v, b0g.at[slot], plane_peer(k))
+    for peer in plane_peers():
+        send(2, b0v, b0g.at[slot], peer)
 
     r1[core * NZ + n] = s1[core, n]
     await_all(rcv.at[1], f3g.at[pl.ds(0, NZ - 1)])
@@ -217,7 +223,7 @@
         last = jnp.concatenate([partial[8 * s : 8 * s + 8, 128:144]] * 8, axis=1)
         gp[s, 8:9] = jnp.sum(jnp.where(lane // 16 == lax.rem(8 - row, 8), last, 0.0), axis=0, keepdims=True)
 
-    @pl.loop(1, 2 * NZ)
+    @pl.loop(0, 2 * NZ - 1)
     def _(k):
         to_w, to_n = column_peer(k)
         send(
@@ -232,9 +238,8 @@
             total = total + g3[i, part]
         gsum[part] = total * (1.0 / float(RANK * RANK * RANK_FOUR))
 
-    @pl.loop(1, NW)
-    def _(k):
-        send(6, gsum.at[pl.ds(0, 9)], gfull.at[slot, pl.ds(0, 9)], plane_peer(k))
+    for peer in plane_peers():
+        send(6, gsum.at[pl.ds(0, 9)], gfull.at[slot, pl.ds(0, 9)], peer)
 
     gfull[slot, 0:9] = gsum[0:9]
     await_all(rcv.at[2], b0g.at[pl.ds(0, NW - 1)])

time: 55 us -> 52.8 us (0.960)
  Pallas kernels: 53.6 us -> 51.3 us
    pallas_call x1, Pallas kernels: 53.6 us -> 51.3 us  [per_device(): pl.pallas_call(kernel, out_shape=jax.ShapeDtypeStruct((8, 64), f32), in_s...]
where the time goes in v4:
time: 52.8 us; the launch traced here: 52.6 us
  Pallas kernels  51.3 us (97%)
  local copies, waits for them, and re-layouts  1.28 us (2%)
    pallas_call x1, Pallas kernels, per_device(): pl.pallas_call(kernel, out_shape=jax.ShapeDtypeStruct((8, 64), f32), in_s...  51.3 us
    unnamed x1, local copies, waits for them, and re-layouts  1.28 us

profile of v4, /device:TPU:1, one launch (start us, length us, event | category | flops | bytes accessed | tf_op | source)
XLA Modules:
  0.0 52.6 jit_solution(9133098551938335167)
XLA Ops:
  0.0 51.3 %hooi.1 = f32[8,64]{1,0:T(8,128)} custom-call(f32[4096,128]{1,0:T(8,128)} %bitcast.6, f32[32,64]{1,0:T(8,128)} %f2_hbm.1, f32[16,64]{1,0:T(8,128)} %f3_hbm.1, f32[2,4]{1,0:T(2,128)} %bitcast.7, f32[8,64]{1,0:T(8,128)} %b0_hbm.1), custom_call_target="tpu_custom_call" | custom-call | tf_op jit(solution)/shard_map/hooi/pallas_call | solution.py:298
  51.3 1.3 %copy.8 = f32[8,64]{1,0:T(8,128)} copy(f32[8,64]{1,0:T(8,128)} %hooi.1) | data formatting | bytes 4096

commit v5 on v4

--- a/solution.py
+++ b/solution.py
@@ -14,7 +14,6 @@
 NW, NZ = 32, 8
 CHIPS = NW // 2
 HALF = CHIPS // 2
-BLOCK = 8
 PLANE = sorted(
     [(x, y, c) for x in range(4) for y in range(4) for c in range(2) if x or y or c],
     key=lambda p: -(min(p[0], 4 - p[0]) + min(p[1], 4 - p[1])),
@@ -41,6 +40,19 @@
     return jnp.dot(a, b, preferred_element_type=jnp.float32)
 
 
+def mm_rows(a, b, dims):
+    def parts(x, y):
+        return lax.dot_general(x, y, (dims, ((), ())), preferred_element_type=jnp.float32)
+
+    ah, am, al = split3(a)
+    bh, bm, bl = split3(b)
+    n = a.shape[0]
+    high = parts(jnp.concatenate([ah, am, al], axis=0), bh)
+    mid = parts(jnp.concatenate([ah, am], axis=0), bm)
+    low = parts(ah, bl)
+    return ((high[2 * n :] + low + mid[n:]) + (high[n : 2 * n] + mid[:n])) + high[:n]
+
+
 def lanes_of(tile, column):
     return jnp.broadcast_to(tile[:, column : column + 1], (8, 128))
 
@@ -49,44 +61,46 @@
     return jnp.broadcast_to(tile[row : row + 1, :], (8, 128))
 
 
-def inverse_cholesky(w):
+def inverse_cholesky(wide):
     row = lax.broadcasted_iota(jnp.int32, (8, 128), 0)
     lane = lax.broadcasted_iota(jnp.int32, (8, 128), 1)
-    wide = jnp.concatenate([w, jnp.zeros((64, 64), jnp.float32)], axis=1)
-    s = []
-    for i in range(8):
-        unit = jnp.where(lane == row + (64 + 8 * i), 1.0, 0.0)
-        s.append(jnp.where(lane < 64, wide[8 * i : 8 * i + 8], unit))
+    s = [
+        wide[8 * i : 8 * i + 8] + jnp.where(lane == row + 8 * i, 1.0, 0.0) for i in range(8)
+    ]
     out = []
+    ahead = [lanes_of(s[0], 64 + q) for q in range(8)]
     for t in range(8):
+        cols = {
+            i: [lanes_of(s[i], 64 + 8 * t + q) for q in range(8)] for i in range(t + 1, 8)
+        }
+        cols[t] = ahead
+        if t < 7:
+            ahead = [lanes_of(s[t + 1], 64 + 8 * (t + 1) + q) for q in range(8)]
         pivots = jnp.ones((8, 128), jnp.float32)
-        for start in range(0, 8, BLOCK):
-            cols = {
-                i: [lanes_of(s[i], 8 * t + start + q) for q in range(BLOCK)]
-                for i in range(t, 8)
-            }
-            for p in range(BLOCK):
-                r = start + p
-                pivot_row = rows_of(s[t], r)
-                pivot = rows_of(cols[t][p], r)
-                inverse = 1.0 / pivot
-                heads = [rows_of(cols[t][q], r) for q in range(BLOCK)]
-                for i in range(t, 8):
-                    factor = cols[i][p] * inverse
-                    if i == t:
-                        factor = jnp.where(row > r, factor, 0.0)
-                    s[i] = s[i] - factor * pivot_row
-                    for q in range(p + 1, BLOCK):
-                        cols[i][q] = cols[i][q] - factor * heads[q]
-                pivots = jnp.where(row == r, pivot, pivots)
+        for p in range(8):
+            pivot_row = rows_of(s[t], p)
+            pivot = rows_of(cols[t][p], p)
+            inverse = 1.0 / pivot
+            heads = [rows_of(cols[t][q], p) for q in range(8)]
+            for i in range(t, 8):
+                factor = cols[i][p] * inverse
+                if i == t:
+                    factor = jnp.where(row > p, factor, 0.0)
+                if i == t + 1:
+                    for q in range(8):
+                        ahead[q] = ahead[q] - factor * rows_of(cols[i][p], q)
+                s[i] = s[i] - factor * pivot_row
+                for q in range(p + 1, 8):
+                    cols[i][q] = cols[i][q] - factor * heads[q]
+            pivots = jnp.where(row == p, pivot, pivots)
         out.append(s[t] * lax.rsqrt(pivots))
-    return jnp.concatenate(out, axis=0)[:, 64:128]
+    return jnp.concatenate(out, axis=0)[:, 0:64]
 
 
 def kernel(
     x_hbm, f2_hbm, f3_hbm, f4_hbm, b0_hbm, out_ref,
     xv, f2v, f3v, f4s, b0v, f2p, f2g, f3g, b0g, yh, ym, yl,
-    s1, r1, vt, v_ref, a_ref, gp, g3, gsum, gfull, gmat, z_ref, linv_ref,
+    s1, r1, vt, v_ref, a_ref, gp, g3, gsum, gfull, gmat, zt_ref, z_ref, linv_ref,
     loc, snd, rcv,
 ):
     w = lax.axis_index("wa")
@@ -243,7 +257,7 @@
 
     gfull[slot, 0:9] = gsum[0:9]
     await_all(rcv.at[2], b0g.at[pl.ds(0, NW - 1)])
-    basis = b0g[...].reshape(256, 64)
+    basis_t = b0g[...].reshape(256, 64).T
     await_all(rcv.at[6], gfull.at[pl.ds(0, NW - 1), pl.ds(0, 9)])
 
     for i in range(CHIPS):
@@ -267,17 +281,17 @@
     column_block = lax.broadcasted_iota(jnp.int32, (256, 256), 1) // 16
     held = lax.rem(column_block - row_block + CHIPS, CHIPS) <= HALF
     gmat[...] = jnp.where(held, half_gram, half_gram.T)
-    z_ref[...] = mm(gmat[...], basis)
+    zt_ref[...] = mm_rows(basis_t, gmat[...], ((1,), (0,)))
 
     @pl.loop(0, ITERS)
     def _(step):
-        z = z_ref[...]
-        linv_ref[...] = inverse_cholesky(mm(z, z, ((0,), (0,))))
-
-        @pl.when(step < ITERS - 1)
-        def _():
-            image = mm(gmat[...], z)
-            z_ref[...] = mm(image, linv_ref[...], ((1,), (1,)))
+        zt = zt_ref[...]
+        below = jnp.concatenate([jnp.zeros((64, 256), jnp.float32), zt], axis=0)
+        linv = inverse_cholesky(mm_rows(zt, below, ((1,), (1,))))
+        linv_ref[...] = linv
+        z_ref[...] = zt.T
+        image_t = mm(zt, gmat[...])
+        zt_ref[...] = mm_rows(linv, image_t, ((1,), (0,)))
 
     mine = z_ref[pl.ds(pl.multiple_of(slot * 8, 8), 8), :]
     out_ref[...] = mm(mine, linv_ref[...], ((1,), (1,))) * math.sqrt(256.0)
@@ -323,6 +337,7 @@
             pltpu.VMEM((16, 128), f32),
             pltpu.VMEM((NW, 16, 128), f32),
             pltpu.VMEM((256, 256), f32),
+            pltpu.VMEM((64, 256), f32),
             pltpu.VMEM((256, 64), f32),
             pltpu.VMEM((64, 64), f32),
             pltpu.SemaphoreType.DMA((5,)),

time: 52.8 us -> 48.7 us (0.922)
  Pallas kernels: 51.3 us -> 47.2 us
    pallas_call x1, Pallas kernels: 51.3 us -> 47.2 us  [per_device(): pl.pallas_call(kernel, out_shape=jax.ShapeDtypeStruct((8, 64), f32), in_s...]
where the time goes in v5:
time: 48.7 us; the launch traced here: 48.5 us
  Pallas kernels  47.2 us (97%)
  local copies, waits for them, and re-layouts  1.28 us (3%)
    pallas_call x1, Pallas kernels, per_device(): pl.pallas_call(kernel, out_shape=jax.ShapeDtypeStruct((8, 64), f32), in_s...  47.2 us
    unnamed x1, local copies, waits for them, and re-layouts  1.28 us

profile of v5, /device:TPU:1, one launch (start us, length us, event | category | flops | bytes accessed | tf_op | source)
XLA Modules:
  0.0 48.5 jit_solution(11384185646697182264)
XLA Ops:
  0.0 47.2 %hooi.1 = f32[8,64]{1,0:T(8,128)} custom-call(f32[4096,128]{1,0:T(8,128)} %bitcast.6, f32[32,64]{1,0:T(8,128)} %f2_hbm.1, f32[16,64]{1,0:T(8,128)} %f3_hbm.1, f32[2,4]{1,0:T(2,128)} %bitcast.7, f32[8,64]{1,0:T(8,128)} %b0_hbm.1), custom_call_target="tpu_custom_call" | custom-call | tf_op jit(solution)/shard_map/hooi/pallas_call | solution.py:312
  47.2 1.3 %copy.8 = f32[8,64]{1,0:T(8,128)} copy(f32[8,64]{1,0:T(8,128)} %hooi.1) | data formatting | bytes 4096

commit v6 on v5

--- a/solution.py
+++ b/solution.py
@@ -14,10 +14,26 @@
 NW, NZ = 32, 8
 CHIPS = NW // 2
 HALF = CHIPS // 2
-PLANE = sorted(
-    [(x, y, c) for x in range(4) for y in range(4) for c in range(2) if x or y or c],
-    key=lambda p: -(min(p[0], 4 - p[0]) + min(p[1], 4 - p[1])),
+def hops(peer):
+    x, y, z, c = peer
+    return min(x, 4 - x) + min(y, 4 - y) + min(z, NZ - z) + 0.5 * c
+
+
+EVERY = sorted(
+    [
+        (x, y, z, c)
+        for x in range(4)
+        for y in range(4)
+        for z in range(NZ)
+        for c in range(2)
+        if (x or y or z or c) and not ((x or y) and z)
+    ],
+    key=hops,
+    reverse=True,
 )
+PLANE = [(x, y, c) for x, y, z, c in EVERY if z == 0]
+
+
 MESH = pl.DeviceIdType.MESH
 HIGHEST = lax.Precision.HIGHEST
 
@@ -133,12 +149,10 @@
         dz = NZ // 2 + reach * (1 - 2 * lax.rem(step, 2))
         return chip * 2 + lax.rem(core + k + 1, 2), lax.rem(n + dz, NZ)
 
-    for peer in plane_peers():
+    for dx, dy, dz, dc in EVERY:
+        to = lax.rem(chip // 4 + dx, 4) * 4 + lax.rem(chip + dy, 4)
+        peer = to * 2 + lax.rem(core + dc, 2), lax.rem(n + dz, NZ)
         pl.semaphore_signal(barrier, inc=1, device_id=peer, device_id_type=MESH)
-
-    @pl.loop(0, 2 * NZ - 2)
-    def _(k):
-        pl.semaphore_signal(barrier, inc=1, device_id=column_peer(k), device_id_type=MESH)
 
     local[0].wait()
     local[1].wait()
@@ -230,7 +244,7 @@
 
     a_ref[0] = v_ref[...]
     await_all(rcv.at[4], a_ref.at[pl.ds(1, HALF)])
-    partial = mm(v_ref[...], a_ref[...].reshape(144, 512), ((1,), (1,)))
+    partial = mm_rows(v_ref[...], a_ref[...].reshape(144, 512), ((1,), (1,)))
     row = lax.broadcasted_iota(jnp.int32, (8, 128), 0)
     for s in range(2):
         gp[s, 0:8] = partial[8 * s : 8 * s + 8, 0:128]
@@ -291,7 +305,10 @@
         linv_ref[...] = linv
         z_ref[...] = zt.T
         image_t = mm(zt, gmat[...])
-        zt_ref[...] = mm_rows(linv, image_t, ((1,), (0,)))
+
+        @pl.when(step < ITERS - 1)
+        def _():
+            zt_ref[...] = mm_rows(linv, image_t, ((1,), (0,)))
 
     mine = z_ref[pl.ds(pl.multiple_of(slot * 8, 8), 8), :]
     out_ref[...] = mm(mine, linv_ref[...], ((1,), (1,))) * math.sqrt(256.0)
@@ -309,6 +326,7 @@
     f32, bf16 = jnp.float32, jnp.bfloat16
     x = tensor.reshape(8, 8, 128, 16, 4).transpose(0, 3, 1, 4, 2).reshape(4096, 128)
     hbm = pl.BlockSpec(memory_space=pltpu.HBM)
+    operands = (x, factor_two, factor_three, factor_four.T, start_basis)
     return pl.pallas_call(
         kernel,
         out_shape=jax.ShapeDtypeStruct((8, 64), f32),
@@ -345,10 +363,10 @@
             pltpu.SemaphoreType.DMA((7,)),
         ],
         compiler_params=pltpu.CompilerParams(
-            collective_id=0, has_side_effects=True, vmem_limit_bytes=60 * 2**20
+            collective_id=0, has_side_effects=True, vmem_limit_bytes=40 * 2**20
         ),
         name="hooi",
-    )(x, factor_two, factor_three, factor_four.T, start_basis)
+    )(*(pltpu.with_memory_space_constraint(v, pltpu.HBM) for v in operands))
 
 
 def solution(mesh):

time: 48.7 us -> 46.6 us (0.957)
  Pallas kernels: 47.2 us -> 45.9 us
  local copies, waits for them, and re-layouts: 1.28 us -> 0.6 us
    pallas_call x1, Pallas kernels: 47.2 us -> 45.9 us  [per_device(): pl.pallas_call(kernel, out_shape=jax.ShapeDtypeStruct((8, 64), f32), in_s...]
    unnamed x1, local copies, waits for them, and re-layouts: 1.28 us -> 0.6 us
where the time goes in v6:
time: 46.6 us; the launch traced here: 46.5 us
  Pallas kernels  45.9 us (98%)
  local copies, waits for them, and re-layouts  0.6 us (1%)
    pallas_call x1, Pallas kernels, per_device(): pl.pallas_call(kernel, out_shape=jax.ShapeDtypeStruct((8, 64), f32), in_s...  45.9 us

profile of v6, /device:TPU:1, one launch (start us, length us, event | category | flops | bytes accessed | tf_op | source)
XLA Modules:
  0.0 46.5 jit_solution(16976521588324388393)
XLA Ops:
  0.0 45.9 %hooi.1 = f32[8,64]{1,0:T(8,128)S(1)} custom-call(f32[4096,128]{1,0:T(8,128)} %bitcast.6, f32[32,64]{1,0:T(8,128)} %f2_hbm.1, f32[16,64]{1,0:T(8,128)} %f3_hbm.1, f32[2,4]{1,0:T(2,128)} %bitcast.7, f32[8,64]{1,0:T(8,128)} %b0_hbm.1), custom_call_target="tpu_custom_call" | custom-call | tf_op jit(solution)/shard_map/hooi/pallas_call | solution.py:330
  45.9 0.6 %copy.8 = f32[8,64]{1,0:T(8,128)} copy(f32[8,64]{1,0:T(8,128)S(1)} %hooi.1) | data formatting | bytes 4096

commit v7 on v6

--- a/solution.py
+++ b/solution.py
@@ -32,6 +32,7 @@
     reverse=True,
 )
 PLANE = [(x, y, c) for x, y, z, c in EVERY if z == 0]
+COLUMN = [(z, c) for x, y, z, c in EVERY if x == 0 and y == 0]
 
 
 MESH = pl.DeviceIdType.MESH
@@ -143,11 +144,10 @@
             to = lax.rem(chip // 4 + dx, 4) * 4 + lax.rem(chip + dy, 4)
             yield to * 2 + lax.rem(core + dc, 2), n
 
-    def column_peer(k):
-        step = k // 2
-        reach = (step + 1) // 2
-        dz = NZ // 2 + reach * (1 - 2 * lax.rem(step, 2))
-        return chip * 2 + lax.rem(core + k + 1, 2), lax.rem(n + dz, NZ)
+    def column_peers():
+        for dz, dc in COLUMN:
+            to = lax.rem(core + dc, 2)
+            yield to, (chip * 2 + to, lax.rem(n + dz, NZ))
 
     for dx, dy, dz, dc in EVERY:
         to = lax.rem(chip // 4 + dx, 4) * 4 + lax.rem(chip + dy, 4)
@@ -196,9 +196,10 @@
             yl[here] = l
 
     await_all(rcv.at[0], f2g.at[pl.ds(0, NW - 1)])
-    packed = f2g[...]
-    full_two = jnp.concatenate([packed[:, :, 0:64], packed[:, :, 64:128]], axis=1)
-    wh, wm, wl = split3(full_two.reshape(1024, 64))
+    wh, wm, wl = (
+        jnp.concatenate([v[:, :, 0:64], v[:, :, 64:128]], axis=1).reshape(1024, 64)
+        for v in split3(f2g[...])
+    )
     p0 = mm16(yh[...], jnp.concatenate([wh, wm, wl], axis=1))
     p1 = mm16(ym[...], jnp.concatenate([wh, wm], axis=1))
     p2 = mm16(yl[...], wh)
@@ -206,10 +207,8 @@
     for g in range(2):
         s1[g] = first[128 * g : 128 * g + 128].T.reshape(8, 8, 128)
 
-    @pl.loop(0, 2 * NZ - 1)
-    def _(k):
-        to_w, to_n = column_peer(k)
-        send(3, s1.at[lax.rem(to_w, 2), to_n], r1.at[core * NZ + n], (to_w, to_n))
+    for to, peer in column_peers():
+        send(3, s1.at[to, peer[1]], r1.at[core * NZ + n], peer)
 
     for peer in plane_peers():
         send(2, b0v, b0g.at[slot], peer)
@@ -237,8 +236,7 @@
     for e in range(8):
         v_ref[:, 64 * e : 64 * e + 64] = vt[pl.ds(e, 16, stride=8), :]
 
-    @pl.loop(1, HALF + 1)
-    def _(k):
+    for k in (1, 3, 6, 2, 5, 7, 8, 4):
         to = lax.rem(7 * lax.rem(label + CHIPS - k, CHIPS), CHIPS)
         send(4, v_ref, a_ref.at[k], (to * 2 + core, n))
 
@@ -251,12 +249,8 @@
         last = jnp.concatenate([partial[8 * s : 8 * s + 8, 128:144]] * 8, axis=1)
         gp[s, 8:9] = jnp.sum(jnp.where(lane // 16 == lax.rem(8 - row, 8), last, 0.0), axis=0, keepdims=True)
 
-    @pl.loop(0, 2 * NZ - 1)
-    def _(k):
-        to_w, to_n = column_peer(k)
-        send(
-            5, gp.at[lax.rem(to_w, 2), pl.ds(0, 9)], g3.at[core * NZ + n, pl.ds(0, 9)], (to_w, to_n)
-        )
+    for to, peer in column_peers():
+        send(5, gp.at[to, pl.ds(0, 9)], g3.at[core * NZ + n, pl.ds(0, 9)], peer)
 
     g3[core * NZ + n, 0:9] = gp[core, 0:9]
     await_all(rcv.at[5], g3.at[pl.ds(0, 2 * NZ - 1), pl.ds(0, 9)])
@@ -303,13 +297,13 @@
         below = jnp.concatenate([jnp.zeros((64, 256), jnp.float32), zt], axis=0)
         linv = inverse_cholesky(mm_rows(zt, below, ((1,), (1,))))
         linv_ref[...] = linv
-        z_ref[...] = zt.T
         image_t = mm(zt, gmat[...])
 
         @pl.when(step < ITERS - 1)
         def _():
             zt_ref[...] = mm_rows(linv, image_t, ((1,), (0,)))
 
+    z_ref[...] = zt_ref[...].T
     mine = z_ref[pl.ds(pl.multiple_of(slot * 8, 8), 8), :]
     out_ref[...] = mm(mine, linv_ref[...], ((1,), (1,))) * math.sqrt(256.0)
 

time: 46.6 us -> 46.7 us (level)
  no operation moved by 1% of the time
where the time goes in v7:
time: 46.7 us; the launch traced here: 46.5 us
  Pallas kernels  45.9 us (98%)
  local copies, waits for them, and re-layouts  0.6 us (1%)
    pallas_call x1, Pallas kernels, per_device(): pl.pallas_call(kernel, out_shape=jax.ShapeDtypeStruct((8, 64), f32), in_s...  45.9 us

profile of v7, /device:TPU:1, one launch (start us, length us, event | category | flops | bytes accessed | tf_op | source)
XLA Modules:
  0.0 46.5 jit_solution(14533355020528706680)
XLA Ops:
  0.0 45.9 %hooi.1 = f32[8,64]{1,0:T(8,128)S(1)} custom-call(f32[4096,128]{1,0:T(8,128)} %bitcast.6, f32[32,64]{1,0:T(8,128)} %f2_hbm.1, f32[16,64]{1,0:T(8,128)} %f3_hbm.1, f32[2,4]{1,0:T(2,128)} %bitcast.7, f32[8,64]{1,0:T(8,128)} %b0_hbm.1), custom_call_target="tpu_custom_call" | custom-call | tf_op jit(solution)/shard_map/hooi/pallas_call | solution.py:324
  45.9 0.6 %copy.8 = f32[8,64]{1,0:T(8,128)} copy(f32[8,64]{1,0:T(8,128)S(1)} %hooi.1) | data formatting | bytes 4096

commit v8 on v7

--- a/solution.py
+++ b/solution.py
@@ -57,17 +57,21 @@
     return jnp.dot(a, b, preferred_element_type=jnp.float32)
 
 
+def mm_parts(a, b, dims):
+    def product(x, y):
+        return lax.dot_general(x, y, (dims, ((), ())), preferred_element_type=jnp.float32)
+
+    ah, am, al = a
+    bh, bm, bl = b
+    n = ah.shape[0]
+    high = product(jnp.concatenate([ah, am, al], axis=0), bh)
+    mid = product(jnp.concatenate([ah, am], axis=0), bm)
+    low = product(ah, bl)
+    return ((high[2 * n :] + low + mid[n:]) + (high[n : 2 * n] + mid[:n])) + high[:n]
+
+
 def mm_rows(a, b, dims):
-    def parts(x, y):
-        return lax.dot_general(x, y, (dims, ((), ())), preferred_element_type=jnp.float32)
-
-    ah, am, al = split3(a)
-    bh, bm, bl = split3(b)
-    n = a.shape[0]
-    high = parts(jnp.concatenate([ah, am, al], axis=0), bh)
-    mid = parts(jnp.concatenate([ah, am], axis=0), bm)
-    low = parts(ah, bl)
-    return ((high[2 * n :] + low + mid[n:]) + (high[n : 2 * n] + mid[:n])) + high[:n]
+    return mm_parts(split3(a), split3(b), dims)
 
 
 def lanes_of(tile, column):
@@ -117,7 +121,7 @@
 def kernel(
     x_hbm, f2_hbm, f3_hbm, f4_hbm, b0_hbm, out_ref,
     xv, f2v, f3v, f4s, b0v, f2p, f2g, f3g, b0g, yh, ym, yl,
-    s1, r1, vt, v_ref, a_ref, gp, g3, gsum, gfull, gmat, zt_ref, z_ref, linv_ref,
+    s1, r1, vt, v_ref, a_ref, gp, g3, gsum, gfull, gmat, gparts, zt_ref, z_ref, linv_ref,
     loc, snd, rcv,
 ):
     w = lax.axis_index("wa")
@@ -134,8 +138,7 @@
         pltpu.make_async_copy(f4_hbm, f4s, loc.at[3]),
         pltpu.make_async_copy(x_hbm, xv, loc.at[4]),
     ]
-    for copy in local:
-        copy.start()
+    local[0].start()
 
     barrier = pltpu.get_barrier_semaphore()
 
@@ -154,6 +157,8 @@
         peer = to * 2 + lax.rem(core + dc, 2), lax.rem(n + dz, NZ)
         pl.semaphore_signal(barrier, inc=1, device_id=peer, device_id_type=MESH)
 
+    for copy in local[1:]:
+        copy.start()
     local[0].wait()
     local[1].wait()
     local[2].wait()
@@ -288,16 +293,19 @@
     row_block = lax.broadcasted_iota(jnp.int32, (256, 256), 0) // 16
     column_block = lax.broadcasted_iota(jnp.int32, (256, 256), 1) // 16
     held = lax.rem(column_block - row_block + CHIPS, CHIPS) <= HALF
-    gmat[...] = jnp.where(held, half_gram, half_gram.T)
-    zt_ref[...] = mm_rows(basis_t, gmat[...], ((1,), (0,)))
+    gram = split3(jnp.where(held, half_gram, half_gram.T))
+    for i in range(3):
+        gparts[i] = gram[i]
+    zt_ref[...] = mm_parts(split3(basis_t), gram, ((1,), (0,)))
 
     @pl.loop(0, ITERS)
     def _(step):
         zt = zt_ref[...]
-        below = jnp.concatenate([jnp.zeros((64, 256), jnp.float32), zt], axis=0)
-        linv = inverse_cholesky(mm_rows(zt, below, ((1,), (1,))))
+        z = split3(zt)
+        below = [jnp.concatenate([jnp.zeros((64, 256), v.dtype), v], axis=0) for v in z]
+        linv = inverse_cholesky(mm_parts(z, below, ((1,), (1,))))
         linv_ref[...] = linv
-        image_t = mm(zt, gmat[...])
+        image_t = mm_parts(z, [gparts[i] for i in range(3)], ((1,), (0,)))
 
         @pl.when(step < ITERS - 1)
         def _():
@@ -349,6 +357,7 @@
             pltpu.VMEM((16, 128), f32),
             pltpu.VMEM((NW, 16, 128), f32),
             pltpu.VMEM((256, 256), f32),
+            pltpu.VMEM((3, 256, 256), bf16),
             pltpu.VMEM((64, 256), f32),
             pltpu.VMEM((256, 64), f32),
             pltpu.VMEM((64, 64), f32),

time: 46.7 us -> 46.6 us (level)
  no operation moved by 1% of the time
where the time goes in v8:
time: 46.6 us; the launch traced here: 46.4 us
  Pallas kernels  45.8 us (98%)
  local copies, waits for them, and re-layouts  0.6 us (1%)
    pallas_call x1, Pallas kernels, per_device(): pl.pallas_call(kernel, out_shape=jax.ShapeDtypeStruct((8, 64), f32), in_s...  45.8 us

profile of v8, /device:TPU:1, one launch (start us, length us, event | category | flops | bytes accessed | tf_op | source)
XLA Modules:
  0.0 46.4 jit_solution(9700602107417462353)
XLA Ops:
  0.0 45.8 %hooi.1 = f32[8,64]{1,0:T(8,128)S(1)} custom-call(f32[4096,128]{1,0:T(8,128)} %bitcast.6, f32[32,64]{1,0:T(8,128)} %f2_hbm.1, f32[16,64]{1,0:T(8,128)} %f3_hbm.1, f32[2,4]{1,0:T(2,128)} %bitcast.7, f32[8,64]{1,0:T(8,128)} %b0_hbm.1), custom_call_target="tpu_custom_call" | custom-call | tf_op jit(solution)/shard_map/hooi/pallas_call | solution.py:332
  45.8 0.6 %copy.8 = f32[8,64]{1,0:T(8,128)} copy(f32[8,64]{1,0:T(8,128)S(1)} %hooi.1) | data formatting | bytes 4096

commit v9 on v8

--- a/solution.py
+++ b/solution.py
@@ -164,7 +164,7 @@
     local[2].wait()
     f2p[:, 0:64] = f2v[0:16, :]
     f2p[:, 64:128] = f2v[16:32, :]
-    f2g[w] = f2p[...]
+    f2g[core * CHIPS + chip] = f2p[...]
     f3g[n] = f3v[...]
     b0g[slot] = b0v[...]
 
@@ -179,8 +179,9 @@
     def await_all(sem, blocks):
         pltpu.make_async_copy(blocks, blocks, sem).wait()
 
-    for peer in plane_peers():
-        send(0, f2p, f2g.at[w], peer)
+    for to, peer in zip(PLANE, plane_peers()):
+        if to[2] == 0:
+            send(0, f2p, f2g.at[core * CHIPS + chip], peer)
 
     @pl.loop(1, NZ)
     def _(k):
@@ -200,10 +201,16 @@
             ym[here] = m
             yl[here] = l
 
-    await_all(rcv.at[0], f2g.at[pl.ds(0, NW - 1)])
+    await_all(rcv.at[0], f2g.at[pl.ds(0, CHIPS - 1)])
+    mine = f2g.at[pl.ds(core * CHIPS, CHIPS)]
+    send(7, mine, mine, (chip * 2 + 1 - core, n))
+    await_all(rcv.at[7], f2g.at[pl.ds(0, CHIPS)])
+    halves = [split3(f2g[CHIPS * c : CHIPS * c + CHIPS]) for c in range(2)]
     wh, wm, wl = (
-        jnp.concatenate([v[:, :, 0:64], v[:, :, 64:128]], axis=1).reshape(1024, 64)
-        for v in split3(f2g[...])
+        jnp.concatenate(
+            [v[:, :, 64 * h : 64 * h + 64] for v in pair for h in range(2)], axis=1
+        ).reshape(1024, 64)
+        for pair in zip(*halves)
     )
     p0 = mm16(yh[...], jnp.concatenate([wh, wm, wl], axis=1))
     p1 = mm16(ym[...], jnp.concatenate([wh, wm], axis=1))
@@ -315,7 +322,8 @@
     mine = z_ref[pl.ds(pl.multiple_of(slot * 8, 8), 8), :]
     out_ref[...] = mm(mine, linv_ref[...], ((1,), (1,))) * math.sqrt(256.0)
 
-    await_all(snd.at[0], f2g.at[pl.ds(0, NW - 1)])
+    await_all(snd.at[0], f2g.at[pl.ds(0, CHIPS - 1)])
+    await_all(snd.at[7], f2g.at[pl.ds(0, CHIPS)])
     await_all(snd.at[1], f3g.at[pl.ds(0, NZ - 1)])
     await_all(snd.at[2], b0g.at[pl.ds(0, NW - 1)])
     await_all(snd.at[3], r1.at[pl.ds(0, 2 * NZ - 1)])
@@ -362,8 +370,8 @@
             pltpu.VMEM((256, 64), f32),
             pltpu.VMEM((64, 64), f32),
             pltpu.SemaphoreType.DMA((5,)),
-            pltpu.SemaphoreType.DMA((7,)),
-            pltpu.SemaphoreType.DMA((7,)),
+            pltpu.SemaphoreType.DMA((8,)),
+            pltpu.SemaphoreType.DMA((8,)),
         ],
         compiler_params=pltpu.CompilerParams(
             collective_id=0, has_side_effects=True, vmem_limit_bytes=40 * 2**20

time: 46.6 us -> 46.4 us (level)
  no operation moved by 1% of the time
where the time goes in v9:
time: 46.4 us; the launch traced here: 46.3 us
  Pallas kernels  45.6 us (98%)
  local copies, waits for them, and re-layouts  0.6 us (1%)
    pallas_call x1, Pallas kernels, per_device(): pl.pallas_call(kernel, out_shape=jax.ShapeDtypeStruct((8, 64), f32), in_s...  45.6 us

profile of v9, /device:TPU:1, one launch (start us, length us, event | category | flops | bytes accessed | tf_op | source)
XLA Modules:
  0.0 46.3 jit_solution(9995090035577612282)
XLA Ops:
  0.0 45.6 %hooi.1 = f32[8,64]{1,0:T(8,128)S(1)} custom-call(f32[4096,128]{1,0:T(8,128)} %bitcast.6, f32[32,64]{1,0:T(8,128)} %f2_hbm.1, f32[16,64]{1,0:T(8,128)} %f3_hbm.1, f32[2,4]{1,0:T(2,128)} %bitcast.7, f32[8,64]{1,0:T(8,128)} %b0_hbm.1), custom_call_target="tpu_custom_call" | custom-call | tf_op jit(solution)/shard_map/hooi/pallas_call | solution.py:340
  45.7 0.6 %copy.8 = f32[8,64]{1,0:T(8,128)} copy(f32[8,64]{1,0:T(8,128)S(1)} %hooi.1) | data formatting | bytes 4096

commit v10 on v8

--- a/solution.py
+++ b/solution.py
@@ -160,13 +160,9 @@
     for copy in local[1:]:
         copy.start()
     local[0].wait()
-    local[1].wait()
-    local[2].wait()
     f2p[:, 0:64] = f2v[0:16, :]
     f2p[:, 64:128] = f2v[16:32, :]
     f2g[w] = f2p[...]
-    f3g[n] = f3v[...]
-    b0g[slot] = b0v[...]
 
     pl.semaphore_wait(barrier, NW - 1 + 2 * NZ - 2)
 
@@ -182,9 +178,14 @@
     for peer in plane_peers():
         send(0, f2p, f2g.at[w], peer)
 
+    local[1].wait()
     @pl.loop(1, NZ)
     def _(k):
         send(1, f3v, f3g.at[n], (w, lax.rem(n + k, NZ)))
+
+    local[2].wait()
+    f3g[n] = f3v[...]
+    b0g[slot] = b0v[...]
 
     local[3].wait()
     local[4].wait()

time: 46.6 us -> 46.6 us (level)
  no operation moved by 1% of the time
where the time goes in v10:
time: 46.6 us; the launch traced here: 46.4 us
  Pallas kernels  45.8 us (98%)
  local copies, waits for them, and re-layouts  0.6 us (1%)
    pallas_call x1, Pallas kernels, per_device(): pl.pallas_call(kernel, out_shape=jax.ShapeDtypeStruct((8, 64), f32), in_s...  45.8 us

profile of v10, /device:TPU:1, one launch (start us, length us, event | category | flops | bytes accessed | tf_op | source)
XLA Modules:
  0.0 46.4 jit_solution(14991488518006165911)
XLA Ops:
  0.0 45.8 %hooi.1 = f32[8,64]{1,0:T(8,128)S(1)} custom-call(f32[4096,128]{1,0:T(8,128)} %bitcast.6, f32[32,64]{1,0:T(8,128)} %f2_hbm.1, f32[16,64]{1,0:T(8,128)} %f3_hbm.1, f32[2,4]{1,0:T(2,128)} %bitcast.7, f32[8,64]{1,0:T(8,128)} %b0_hbm.1), custom_call_target="tpu_custom_call" | custom-call | tf_op jit(solution)/shard_map/hooi/pallas_call | solution.py:333
  45.8 0.6 %copy.8 = f32[8,64]{1,0:T(8,128)} copy(f32[8,64]{1,0:T(8,128)S(1)} %hooi.1) | data formatting | bytes 4096

commit v11 on v10

--- a/solution.py
+++ b/solution.py
@@ -98,6 +98,7 @@
         if t < 7:
             ahead = [lanes_of(s[t + 1], 64 + 8 * (t + 1) + q) for q in range(8)]
         pivots = jnp.ones((8, 128), jnp.float32)
+        later = {i: [] for i in range(t + 2, 8)}
         for p in range(8):
             pivot_row = rows_of(s[t], p)
             pivot = rows_of(cols[t][p], p)
@@ -110,10 +111,15 @@
                 if i == t + 1:
                     for q in range(8):
                         ahead[q] = ahead[q] - factor * rows_of(cols[i][p], q)
-                s[i] = s[i] - factor * pivot_row
+                if i < t + 2:
+                    s[i] = s[i] - factor * pivot_row
+                else:
+                    later[i].append(factor * pivot_row)
                 for q in range(p + 1, 8):
                     cols[i][q] = cols[i][q] - factor * heads[q]
             pivots = jnp.where(row == p, pivot, pivots)
+        for i, v in later.items():
+            s[i] = s[i] - (((v[0] + v[1]) + (v[2] + v[3])) + ((v[4] + v[5]) + (v[6] + v[7])))
         out.append(s[t] * lax.rsqrt(pivots))
     return jnp.concatenate(out, axis=0)[:, 0:64]
 
@@ -215,9 +221,6 @@
 
     for to, peer in column_peers():
         send(3, s1.at[to, peer[1]], r1.at[core * NZ + n], peer)
-
-    for peer in plane_peers():
-        send(2, b0v, b0g.at[slot], peer)
 
     r1[core * NZ + n] = s1[core, n]
     await_all(rcv.at[1], f3g.at[pl.ds(0, NZ - 1)])
@@ -257,6 +260,9 @@
 
     for to, peer in column_peers():
         send(5, gp.at[to, pl.ds(0, 9)], g3.at[core * NZ + n, pl.ds(0, 9)], peer)
+
+    for peer in plane_peers():
+        send(2, b0v, b0g.at[slot], peer)
 
     g3[core * NZ + n, 0:9] = gp[core, 0:9]
     await_all(rcv.at[5], g3.at[pl.ds(0, 2 * NZ - 1), pl.ds(0, 9)])

time: 46.6 us -> 46.5 us (level)
  no operation moved by 1% of the time
where the time goes in v11:
time: 46.5 us; the launch traced here: 46.4 us
  Pallas kernels  45.8 us (98%)
  local copies, waits for them, and re-layouts  0.6 us (1%)
    pallas_call x1, Pallas kernels, per_device(): pl.pallas_call(kernel, out_shape=jax.ShapeDtypeStruct((8, 64), f32), in_s...  45.8 us

profile of v11, /device:TPU:1, one launch (start us, length us, event | category | flops | bytes accessed | tf_op | source)
XLA Modules:
  0.0 46.4 jit_solution(2544350750136468782)
XLA Ops:
  0.0 45.8 %hooi.1 = f32[8,64]{1,0:T(8,128)S(1)} custom-call(f32[4096,128]{1,0:T(8,128)} %bitcast.6, f32[32,64]{1,0:T(8,128)} %f2_hbm.1, f32[16,64]{1,0:T(8,128)} %f3_hbm.1, f32[2,4]{1,0:T(2,128)} %bitcast.7, f32[8,64]{1,0:T(8,128)} %b0_hbm.1), custom_call_target="tpu_custom_call" | custom-call | tf_op jit(solution)/shard_map/hooi/pallas_call | solution.py:339
  45.8 0.6 %copy.8 = f32[8,64]{1,0:T(8,128)} copy(f32[8,64]{1,0:T(8,128)S(1)} %hooi.1) | data formatting | bytes 4096

commit v12 on v11

--- a/solution.py
+++ b/solution.py
@@ -222,6 +222,9 @@
     for to, peer in column_peers():
         send(3, s1.at[to, peer[1]], r1.at[core * NZ + n], peer)
 
+    for peer in plane_peers():
+        send(2, b0v, b0g.at[slot], peer)
+
     r1[core * NZ + n] = s1[core, n]
     await_all(rcv.at[1], f3g.at[pl.ds(0, NZ - 1)])
     full_three = f3g[...].reshape(128, 64)
@@ -260,9 +263,6 @@
 
     for to, peer in column_peers():
         send(5, gp.at[to, pl.ds(0, 9)], g3.at[core * NZ + n, pl.ds(0, 9)], peer)
-
-    for peer in plane_peers():
-        send(2, b0v, b0g.at[slot], peer)
 
     g3[core * NZ + n, 0:9] = gp[core, 0:9]
     await_all(rcv.at[5], g3.at[pl.ds(0, 2 * NZ - 1), pl.ds(0, 9)])

time: 46.5 us -> 46.6 us (level)
  no operation moved by 1% of the time
where the time goes in v12:
time: 46.6 us; the launch traced here: 46.4 us
  Pallas kernels  45.8 us (98%)
  local copies, waits for them, and re-layouts  0.6 us (1%)
    pallas_call x1, Pallas kernels, per_device(): pl.pallas_call(kernel, out_shape=jax.ShapeDtypeStruct((8, 64), f32), in_s...  45.8 us

profile of v12, /device:TPU:1, one launch (start us, length us, event | category | flops | bytes accessed | tf_op | source)
XLA Modules:
  0.0 46.4 jit_solution(17081475484636417905)
XLA Ops:
  0.0 45.8 %hooi.1 = f32[8,64]{1,0:T(8,128)S(1)} custom-call(f32[4096,128]{1,0:T(8,128)} %bitcast.6, f32[32,64]{1,0:T(8,128)} %f2_hbm.1, f32[16,64]{1,0:T(8,128)} %f3_hbm.1, f32[2,4]{1,0:T(2,128)} %bitcast.7, f32[8,64]{1,0:T(8,128)} %b0_hbm.1), custom_call_target="tpu_custom_call" | custom-call | tf_op jit(solution)/shard_map/hooi/pallas_call | solution.py:339
  45.8 0.6 %copy.8 = f32[8,64]{1,0:T(8,128)} copy(f32[8,64]{1,0:T(8,128)S(1)} %hooi.1) | data formatting | bytes 4096
